TPU v7x, 32 devices: a whole 2x2x4 slice. The times are simulated.
32 devices in a mesh: dp: 8 (over y, x, core), tensor: 4 (over z).
Axes of the slice: x: 2, y: 2, z: 4, core: 2. Of those that a mesh axis runs over, the one named last changes fastest.
Arguments:
- layer_input: bfloat16 [8192, 1024], P(('dp', 'tensor')), may hold values from -6 to 6
- query_weight: bfloat16 [1024, 1024], P('dp', 'tensor'), may hold values from -0.1875 to 0.1875
- key_weight: bfloat16 [1024, 1024], P('dp', 'tensor'), may hold values from -0.1875 to 0.1875
- value_weight: bfloat16 [1024, 1024], P('dp', 'tensor'), may hold values from -0.1875 to 0.1875
- mixing_weight: bfloat16 [1024, 1024], P('tensor', 'dp'), may hold values from -1.5 to 1.5
- expand_weight: bfloat16 [1024, 4096], P('dp', 'tensor'), may hold values from -0.1875 to 0.1875
- shrink_weight: bfloat16 [4096, 1024], P('tensor', 'dp'), may hold values from -0.09375 to 0.09375
- query_offset: bfloat16 [1024], P('tensor'), may hold values from -3 to 3
- value_offset: bfloat16 [1024], P('tensor'), may hold values from -3 to 3
- mixing_offset: bfloat16 [1024], replicated, may hold values from -2 to 2
- expand_offset: bfloat16 [4096], P('tensor'), may hold values from -3 to 3
- shrink_offset: bfloat16 [1024], replicated, may hold values from -2 to 2
- first_gain: bfloat16 [1024], replicated, may hold values from 0.25 to 1.75
- first_shift: bfloat16 [1024], replicated, may hold values from -2 to 2
- second_gain: bfloat16 [1024], replicated, may hold values from 0.25 to 1.75
- second_shift: bfloat16 [1024], replicated, may hold values from -2 to 2
- cotangent: bfloat16 [8192, 1024], P(('dp', 'tensor')), may hold values from -6 to 6
Outputs:
- layer_output: bfloat16 [8192, 1024], P(('dp', 'tensor'))
- input_grad: float32 [8192, 1024], P(('dp', 'tensor'))
- query_grad: float32 [1024, 1024], P('dp', 'tensor')
- key_grad: float32 [1024, 1024], P('dp', 'tensor')
- value_grad: float32 [1024, 1024], P('dp', 'tensor')
- mixing_grad: float32 [1024, 1024], P('tensor', 'dp')
- expand_grad: float32 [1024, 4096], P('dp', 'tensor')
- shrink_grad: float32 [4096, 1024], P('tensor', 'dp')
- offset_query: float32 [1024], P('tensor')
- offset_value: float32 [1024], P('tensor')
- offset_mixing: float32 [1024], replicated
- offset_expand: float32 [4096], P('tensor')
- offset_shrink: float32 [1024], replicated
- gain_first: float32 [1024], replicated
- shift_first: float32 [1024], replicated
- gain_second: float32 [1024], replicated
- shift_second: float32 [1024], replicated
All inputs are finite; a program needn't handle non-finite values.
Results may differ from a plain program's by a relative error of at most 0.015.
Values may be sent and summed in bfloat16 or wider, within the bound.
A program may use at most 128 MiB of HBM per device.

v0:
```python
import jax
import jax.numpy as jnp
from jax import lax
from jax.sharding import PartitionSpec as P

HD = 64
EPSILON = 1e-05
CONTRACT_ROWS = (((0,), (0,)), ((), ()))
CONTRACT_LAST = (((1,), (1,)), ((), ()))


def layer_norm(inputs, gain, shift):
    centered = inputs - jnp.mean(inputs, axis=-1, keepdims=True)
    variance = jnp.mean(centered * centered, axis=-1, keepdims=True)
    return centered * lax.rsqrt(variance + EPSILON) * gain + shift


def product(left, right):
    return jnp.dot(left, right, preferred_element_type=jnp.float32)


def product_rows(left, right):
    return lax.dot_general(left, right, CONTRACT_ROWS, preferred_element_type=jnp.float32)


def product_last(left, right):
    return lax.dot_general(left, right, CONTRACT_LAST, preferred_element_type=jnp.float32)


def gelu_exact(argument):
    return jax.nn.gelu(argument, approximate=False)


def attend_forward(queries, key_rows, values, block_rows):
    length, heads_here, head_size = queries.shape
    block_count = length // block_rows

    def one_block(query_block):
        scores = jnp.einsum(
            "qhd,khd->hqk", query_block, key_rows, preferred_element_type=jnp.float32
        )
        largest = jnp.max(scores, axis=-1, keepdims=True)
        weights = jnp.exp(scores - largest)
        exp_total = jnp.sum(weights, axis=-1, keepdims=True)
        probs_low = (weights / exp_total).astype(jnp.bfloat16)
        mixture = jnp.einsum("hqk,khd->qhd", probs_low, values, preferred_element_type=jnp.float32)
        log_total = (largest + jnp.log(exp_total))[..., 0]
        return (mixture.astype(jnp.bfloat16), log_total)

    mixture, log_totals = lax.map(
        one_block, queries.reshape(block_count, block_rows, heads_here, head_size)
    )
    return (mixture.reshape(length, heads_here * head_size), log_totals)


def attend_backward(queries, key_rows, values, mixture_low, log_totals, block_rows):
    length, heads_here, head_size = queries.shape
    block_count = length // block_rows

    def one_block(accumulated, inputs):
        key_sum, value_sum = accumulated
        query_block, grad_block, log_block = inputs
        scores = jnp.einsum(
            "qhd,khd->hqk", query_block, key_rows, preferred_element_type=jnp.float32
        )
        probability = jnp.exp(scores - log_block[..., None])
        probs_low = probability.astype(jnp.bfloat16)
        value_sum = value_sum + jnp.einsum(
            "hqk,qhd->khd", probs_low, grad_block, preferred_element_type=jnp.float32
        )
        prob_grad = jnp.einsum(
            "qhd,khd->hqk", grad_block, values, preferred_element_type=jnp.float32
        )
        inner_sum = jnp.sum(prob_grad * probability, axis=-1, keepdims=True)
        score_low = (probability * (prob_grad - inner_sum)).astype(jnp.bfloat16)
        query_low = jnp.einsum(
            "hqk,khd->qhd", score_low, key_rows, preferred_element_type=jnp.float32
        )
        key_sum = key_sum + jnp.einsum(
            "hqk,qhd->khd", score_low, query_block, preferred_element_type=jnp.float32
        )
        return ((key_sum, value_sum), query_low.astype(jnp.bfloat16))

    zeros = jnp.zeros((length, heads_here, head_size), jnp.float32)
    blocked = (length // block_count, heads_here, head_size)
    (key_sum, value_sum), query_low = lax.scan(
        one_block,
        (zeros, zeros),
        (
            queries.reshape((block_count,) + blocked),
            mixture_low.reshape((block_count,) + blocked),
            log_totals,
        ),
    )
    width_here = heads_here * head_size
    return (
        query_low.reshape(length, width_here),
        key_sum.astype(jnp.bfloat16).reshape(length, width_here),
        value_sum.astype(jnp.bfloat16).reshape(length, width_here),
    )


def body(
    layer_input,
    query_weight,
    key_weight,
    value_weight,
    mixing_weight,
    expand_weight,
    shrink_weight,
    query_offset,
    value_offset,
    mixing_offset,
    expand_offset,
    shrink_offset,
    first_gain,
    first_shift,
    second_gain,
    second_shift,
    cotangent,
):
    local_rows = layer_input.shape[0]
    tensor_size = lax.axis_size("tensor")
    length = local_rows * tensor_size
    block_rows = min(512, length)
    heads_here = query_weight.shape[1] // HD
    scaling = HD ** (-0.5)
    head_shape = (length, heads_here, HD)
    gathered = (
        lax.all_gather(query_weight, "dp", axis=0, tiled=True),
        lax.all_gather(key_weight, "dp", axis=0, tiled=True),
        lax.all_gather(value_weight, "dp", axis=0, tiled=True),
        lax.all_gather(mixing_weight, "dp", axis=1, tiled=True),
        lax.all_gather(expand_weight, "dp", axis=0, tiled=True),
        lax.all_gather(shrink_weight, "dp", axis=1, tiled=True),
    )
    query_full, key_full, value_full, mixing_full, expand_full, shrink_full = gathered
    sequence = lax.all_gather(layer_input, "tensor", axis=0, tiled=True)
    queries = ((product(sequence, query_full) + query_offset.astype(jnp.float32)) * scaling).astype(
        jnp.bfloat16
    )
    key_rows = product(sequence, key_full).astype(jnp.bfloat16)
    values = (product(sequence, value_full) + value_offset.astype(jnp.float32)).astype(jnp.bfloat16)
    mixture, log_totals = attend_forward(
        queries.reshape(head_shape),
        key_rows.reshape(head_shape),
        values.reshape(head_shape),
        block_rows,
    )
    attended_part = lax.psum_scatter(
        product(mixture, mixing_full).astype(jnp.bfloat16),
        "tensor",
        scatter_dimension=0,
        tiled=True,
    )
    attended = layer_input.astype(jnp.float32) + attended_part + mixing_offset.astype(jnp.float32)
    first_norm, first_back = jax.vjp(
        layer_norm, attended, first_gain.astype(jnp.float32), first_shift.astype(jnp.float32)
    )
    normed = lax.all_gather(first_norm.astype(jnp.bfloat16), "tensor", axis=0, tiled=True)
    expanded = product(normed, expand_full) + expand_offset.astype(jnp.float32)
    hidden_act, gelu_back = jax.vjp(gelu_exact, expanded)
    hidden = hidden_act.astype(jnp.bfloat16)
    shrunk = lax.psum_scatter(
        product(hidden, shrink_full).astype(jnp.bfloat16), "tensor", scatter_dimension=0, tiled=True
    )
    summed = first_norm + shrunk + shrink_offset.astype(jnp.float32)
    normalized, second_back = jax.vjp(
        layer_norm, summed, second_gain.astype(jnp.float32), second_shift.astype(jnp.float32)
    )
    summed_grad, gain_second, shift_second = second_back(cotangent.astype(jnp.float32))
    query_back, key_back, value_back, mixing_back, expand_back, shrink_back = gathered
    branch_rows = lax.all_gather(summed_grad.astype(jnp.bfloat16), "tensor", axis=0, tiled=True)
    shrink_local = product_rows(hidden, branch_rows)
    hidden_grad = product_last(branch_rows, shrink_back)
    expanded_low = gelu_back(hidden_grad)[0].astype(jnp.bfloat16)
    expand_sum = jnp.sum(expanded_low.astype(jnp.float32), axis=0)
    expand_local = product_rows(normed, expanded_low)
    first_grad = (
        lax.psum_scatter(
            product_last(expanded_low, expand_back).astype(jnp.bfloat16),
            "tensor",
            scatter_dimension=0,
            tiled=True,
        )
        + summed_grad
    )
    shrink_sum = jnp.sum(summed_grad, axis=0)
    attended_grad, gain_first, shift_first = first_back(first_grad)
    mixing_sum = jnp.sum(attended_grad, axis=0)
    attended_rows = lax.all_gather(attended_grad.astype(jnp.bfloat16), "tensor", axis=0, tiled=True)
    mixing_local = product_rows(mixture, attended_rows)
    mixture_low = product_last(attended_rows, mixing_back).astype(jnp.bfloat16)
    query_low, key_low, value_low = attend_backward(
        queries.reshape(head_shape),
        key_rows.reshape(head_shape),
        values.reshape(head_shape),
        mixture_low,
        log_totals,
        block_rows,
    )
    query_local = product_rows(sequence, query_low) * scaling
    key_local = product_rows(sequence, key_low)
    value_local = product_rows(sequence, value_low)
    query_sum = jnp.sum(query_low.astype(jnp.float32), axis=0) * scaling
    value_sum = jnp.sum(value_low.astype(jnp.float32), axis=0)
    input_grad = (
        lax.psum_scatter(
            (
                product_last(query_low, query_back) * scaling
                + product_last(key_low, key_back)
                + product_last(value_low, value_back)
            ).astype(jnp.bfloat16),
            "tensor",
            scatter_dimension=0,
            tiled=True,
        ).astype(jnp.float32)
        + attended_grad
    )
    query_grad, key_grad, value_grad, mixing_grad, expand_grad, shrink_grad = (
        lax.psum_scatter(
            query_local.astype(jnp.bfloat16), "dp", scatter_dimension=0, tiled=True
        ).astype(jnp.float32),
        lax.psum_scatter(
            key_local.astype(jnp.bfloat16), "dp", scatter_dimension=0, tiled=True
        ).astype(jnp.float32),
        lax.psum_scatter(
            value_local.astype(jnp.bfloat16), "dp", scatter_dimension=0, tiled=True
        ).astype(jnp.float32),
        lax.psum_scatter(
            mixing_local.astype(jnp.bfloat16), "dp", scatter_dimension=1, tiled=True
        ).astype(jnp.float32),
        lax.psum_scatter(
            expand_local.astype(jnp.bfloat16), "dp", scatter_dimension=0, tiled=True
        ).astype(jnp.float32),
        lax.psum_scatter(
            shrink_local.astype(jnp.bfloat16), "dp", scatter_dimension=1, tiled=True
        ).astype(jnp.float32),
    )
    tensor_index = lax.axis_index("tensor")
    selector = (jnp.arange(tensor_size)[:, None] == tensor_index).astype(jnp.float32)

    def spread_out(vector):
        return (selector * vector[None, :]).reshape(-1)

    totals = lax.psum(
        (
            gain_first,
            shift_first,
            gain_second,
            shift_second,
            mixing_sum,
            shrink_sum,
            spread_out(query_sum),
            spread_out(value_sum),
            spread_out(expand_sum),
        ),
        ("dp", "tensor"),
    )

    def own_slice(full_vector, slice_size):
        return lax.dynamic_slice_in_dim(full_vector, tensor_index * slice_size, slice_size, 0)

    offset_query = own_slice(totals[6], query_sum.shape[0])
    offset_value = own_slice(totals[7], value_sum.shape[0])
    offset_expand = own_slice(totals[8], expand_sum.shape[0])
    return (
        normalized.astype(jnp.bfloat16),
        input_grad,
        query_grad,
        key_grad,
        value_grad,
        mixing_grad,
        expand_grad,
        shrink_grad,
        offset_query,
        offset_value,
        totals[4],
        offset_expand,
        totals[5],
        totals[0],
        totals[1],
        totals[2],
        totals[3],
    )


def solution(mesh):
    placed = (
        P(("dp", "tensor"), None),
        P("dp", "tensor"),
        P("dp", "tensor"),
        P("dp", "tensor"),
        P("tensor", "dp"),
        P("dp", "tensor"),
        P("tensor", "dp"),
        P("tensor"),
        P("tensor"),
        P(),
        P("tensor"),
        P(),
        P(),
        P(),
        P(),
        P(),
        P(("dp", "tensor"), None),
    )
    return jax.shard_map(
        body,
        mesh=mesh,
        in_specs=placed,
        out_specs=(
            P(("dp", "tensor"), None),
            P(("dp", "tensor"), None),
            P("dp", "tensor"),
            P("dp", "tensor"),
            P("dp", "tensor"),
            P("tensor", "dp"),
            P("dp", "tensor"),
            P("tensor", "dp"),
            P("tensor"),
            P("tensor"),
            P(),
            P("tensor"),
            P(),
            P(),
            P(),
            P(),
            P(),
        ),
        check_vma=False,
    )
```

profile of v0, /device:TPU:0, one launch (start us, length us, event | category | flops | bytes accessed | tf_op | source)
XLA Modules:
  0.0 704.7 jit_solution(7860083018517622834)
XLA Ops:
  10.1 11.6 %all_gather.31 = bf16[1024,256]{1,0:T(8,128)(2,1)S(1)} all-gather(bf16[128,256]{1,0:T(8,128)(2,1)} %param.22), channel_id=1, replica_groups=mesh['dp'=8,'tensor'=4] {'dp'}, dimensions={0}, use_global_device_ids=true | all-gather | bytes 589824 | tf_op jit(solution)/shard_map/all_gather | solution.py:130
  21.7 9.5 %all_gather.32 = bf16[1024,256]{1,0:T(8,128)(2,1)S(1)} all-gather(bf16[128,256]{1,0:T(8,128)(2,1)} %param.23), channel_id=1, replica_groups=mesh['dp'=8,'tensor'=4] {'dp'}, dimensions={0}, use_global_device_ids=true | all-gather | bytes 589824 | tf_op jit(solution)/shard_map/all_gather | solution.py:131
  31.3 9.2 %all_gather.33 = bf16[1024,256]{1,0:T(8,128)(2,1)S(1)} all-gather(bf16[128,256]{1,0:T(8,128)(2,1)} %param.24), channel_id=1, replica_groups=mesh['dp'=8,'tensor'=4] {'dp'}, dimensions={0}, use_global_device_ids=true | all-gather | bytes 589824 | tf_op jit(solution)/shard_map/all_gather | solution.py:132
  40.4 10.9 %all_gather.34 = bf16[256,1024]{1,0:T(8,128)(2,1)} all-gather(bf16[256,128]{1,0:T(8,128)(2,1)} %param.25), channel_id=1, replica_groups=mesh['dp'=8,'tensor'=4] {'dp'}, dimensions={1}, use_global_device_ids=true | all-gather | bytes 589824 | tf_op jit(solution)/shard_map/all_gather | solution.py:133
  51.3 7.8 %all-gather.7.cloned.1.call-done = bf16[1024,1024]{1,0:T(8,128)(2,1)} async-done(((bf16[256,1024]{1,0:T(8,128)(2,1)}), bf16[1024,1024]{1,0:T(8,128)(2,1)}) %all-gather.7.cloned.1.call-update) | async-done | bytes 2097168 | tf_op jit(solution)/shard_map/all_gather | solution.py:138
  59.1 2.3 fusion.43
  62.5 2.3 convolution_convert_fusion.10
  64.8 3.1 fusion.44
  68.0 12.4 %while.27 = (s32[]{:T(128)}, bf16[2,512,4,64]{1,3,2,0:T(8,128)(2,1)S(1)}, f32[2,4,512]{2,1,0:T(4,128)S(1)}, bf16[2,512,4,64]{1,3,2,0:T(8,128)(2,1)S(1)}, bf16[10...) while((s32[]{:T(128)}, bf16[2,512,4,64]{1,3,2,0:T(8,128)(2,1)S(1)}, ...), condition=%wide.region_3.4_spmd, body=%wide.region_0.3_spmd.sunk | while | flops 549582848 | bytes 26804320 | solution.py:50
  68.1 1.4 fusion.129
  69.4 1.7 fusion.130
  71.2 3.0 fusion.131
  74.2 1.4 fusion.129
  75.6 1.7 fusion.130
  77.4 3.0 fusion.131
  81.1 2.0 convolution_convert_fusion.5
  83.9 42.1 %reduce-scatter.21.cloned.1.call-done = bf16[256,1024]{1,0:T(8,128)(2,1)} async-done(((bf16[1024,1024]{1,0:T(8,128)(2,1)}), bf16[256,1024]{1,0:T(8,128)(2,1)}) %reduce-scatter.21.cloned.1.call-update) | async-done | bytes 524304 | tf_op jit(solution)/shard_map/reduce_scatter | solution.py:150
  128.6 2.2 fusion.55
  132.0 43.8 %all-gather.9.cloned.1.call-done = bf16[1024,1024]{1,0:T(8,128)(2,1)} async-done(((bf16[256,1024]{1,0:T(8,128)(2,1)}), bf16[1024,1024]{1,0:T(8,128)(2,1)}) %all-gather.9.cloned.1.call-update) | async-done | bytes 2097168 | tf_op jit(solution)/shard_map/all_gather | solution.py:160
  175.8 14.9 %multiply_convert_fusion.1 = (bf16[1024,1024]{1,0:T(8,128)(2,1)}, f32[1024,1024]{1,0:T(8,128)}, f32[1024,1024]{1,0:T(8,128)}) fusion(f32[1024]{0:T(1024)S(1)} %convert_element_type.190, bf16[1024,1024]{1,0:T(8,128)(2,1)} %all-gather.9.cloned.1.call-done, bf16[1024,1024]{1,0:T(8,128)(2,1)} %all-gather.11.cloned.1.call-done), kind=kOutput, calls=%fused_computation.45 | convolution fusion | flops 2216689664 | bytes 14684160 | tf_op jit(solution)/shard_map/dot_general | solution.py:19
  190.6 13.9 %all-gather.13.cloned.1.call-done = bf16[1024,1024]{1,0:T(8,128)(2,1)} async-done(((bf16[1024,128]{1,0:T(8,128)(2,1)}), bf16[1024,1024]{1,0:T(8,128)(2,1)}) %all-gather.13.cloned.1.call-update) | async-done | bytes 2097168 | tf_op jit(solution)/shard_map/all_gather | solution.py:135
  204.5 6.0 convolution_convert_fusion.4
  210.6 43.9 %reduce-scatter.23.cloned.1.call-done = bf16[256,1024]{1,0:T(8,128)(2,1)} async-done(((bf16[1024,1024]{1,0:T(8,128)(2,1)}), bf16[256,1024]{1,0:T(8,128)(2,1)}) %reduce-scatter.23.cloned.1.call-update) | async-done | bytes 524304 | tf_op jit(solution)/shard_map/reduce_scatter | solution.py:164
  254.5 1.6 fusion.61
  256.9 2.3 fusion.60
  260.3 44.8 %all-gather.15.cloned.1.call-done = bf16[1024,1024]{1,0:T(8,128)(2,1)} async-done(((bf16[256,1024]{1,0:T(8,128)(2,1)}), bf16[1024,1024]{1,0:T(8,128)(2,1)}) %all-gather.15.cloned.1.call-update) | async-done | bytes 2097168 | tf_op jit(solution)/shard_map/all_gather | solution.py:173
  305.1 8.5 %convert_reduce_fusion = (f32[1024]{0:T(1024)S(1)}, bf16[1024,1024]{1,0:T(8,128)(2,1)S(1)}) fusion(f32[1024,1024]{1,0:T(8,128)} %get-tuple-element.287, f32[1024,1024]{1,0:T(8,128)} %get-tuple-element.297, f32[1024]{0:T(1024)S(1)} %convert_element_type.190, bf16[1024,1024]{1,0:T(8,128)(2,1)} %all-gather.15.cloned.1.call-done, ...), kind=kOutput, calls=%fused_computation.42 | convolution fusion | flops 2165308416 | bytes 14688256 | tf_op jit(solution)/shard_map/dot_general | solution.py:27
  315.0 3.7 convolution_convert_fusion.3
  318.7 42.8 %reduce-scatter.25.cloned.1.call-done = bf16[256,1024]{1,0:T(8,128)(2,1)} async-done(((bf16[1024,1024]{1,0:T(8,128)(2,1)}), bf16[256,1024]{1,0:T(8,128)(2,1)}) %reduce-scatter.25.cloned.1.call-update) | async-done | bytes 524304 | tf_op jit(solution)/shard_map/reduce_scatter | solution.py:180
  361.5 1.7 multiply_reduce_fusion.1
  363.3 1.7 fusion.59
  367.0 4.6 convolution_convert_fusion.1
  371.6 2.6 copy.70
  374.2 6.1 convolution_convert_fusion.2
  380.6 31.3 %all-gather.17.cloned.1.call-done = bf16[1024,1024]{1,0:T(8,128)(2,1)} async-done(((bf16[256,1024]{1,0:T(8,128)(2,1)}), bf16[1024,1024]{1,0:T(8,128)(2,1)}) %all-gather.17.cloned.1.call-update) | async-done | bytes 2097168 | tf_op jit(solution)/shard_map/all_gather | solution.py:191
  411.9 3.3 convolution_convert_fusion.6
  415.2 2.1 copy.68
  417.3 3.2 convolution_convert_fusion.9
  420.5 2.8 reshape.191
  423.2 2.3 copy.55
  426.4 21.4 %while.28 = (s32[]{:T(128)}, f32[1024,4,64]{0,2,1:T(8,128)S(1)}, f32[1024,4,64]{0,2,1:T(8,128)S(1)}, bf16[2,512,4,64]{1,3,2,0:T(8,128)(2,1)}, bf16[2,512,4,64]{1...) while((s32[]{:T(128)}, f32[1024,4,64]{0,2,1:T(8,128)S(1)}, ...), condition=%wide.region_17.18_spmd.clone, body=%wide.region_15.17_spmd.clone.sunk | while | flops 1362229248 | bytes 76341480 | solution.py:86
  427.8 1.8 fusion.143
  429.6 3.3 multiply_reduce_fusion.6
  432.9 1.8 multiply_convert_fusion.3
  434.7 1.4 fusion.144
  438.5 1.8 fusion.143
  440.3 3.3 multiply_reduce_fusion.6
  443.6 1.8 multiply_convert_fusion.3
  445.4 1.4 fusion.144
  447.8 1.6 copy.56
  449.5 2.5 fusion.48
  453.2 2.3 fusion.49
  456.7 2.3 fusion.50
  460.1 2.7 fusion.65
  463.9 1.6 copy-done.3
  465.5 2.1 add_convert_fusion
  469.8 29.9 %reduce-scatter.29.cloned.1.call-done = bf16[128,1024]{1,0:T(8,128)(2,1)} async-done(((bf16[1024,1024]{1,0:T(8,128)(2,1)}), bf16[128,1024]{1,0:T(8,128)(2,1)}) %reduce-scatter.29.cloned.1.call-update) | async-done | bytes 262160 | tf_op jit(solution)/shard_map/reduce_scatter | solution.py:233
  499.8 1.8 convert_element_type.221
  502.0 40.7 %all-reduce = (f32[1024]{0:T(1024)S(1)}, f32[1024]{0:T(1024)S(1)}, f32[1024]{0:T(1024)}, f32[4096]{0:T(1024)S(1)}, f32[1024]{0:T(1024)}, /*index=5*/f32[1024]{0:...) all-reduce(f32[1024]{0:T(1024)S(1)} %bitcast.175, ...), channel_id=1, replica_groups=mesh['dp'=8,'tensor'=4] {'dp','tensor'}, use_global_device_ids=true, to_apply=%region_26.27 | all-reduce | flops 12288 | bytes 98304 | tf_op jit(solution)/shard_map/psum | solution.py:246
  546.2 28.1 %reduce-scatter.31.cloned.1.call-done = bf16[128,256]{1,0:T(8,128)(2,1)} async-done(((bf16[1024,256]{1,0:T(8,128)(2,1)}), bf16[128,256]{1,0:T(8,128)(2,1)}) %reduce-scatter.31.cloned.1.call-update) | async-done | bytes 65552
  576.1 35.8 %reduce-scatter.33.cloned.1.call-done = bf16[128,256]{1,0:T(8,128)(2,1)} async-done(((bf16[1024,256]{1,0:T(8,128)(2,1)}), bf16[128,256]{1,0:T(8,128)(2,1)}) %reduce-scatter.33.cloned.1.call-update) | async-done | bytes 65552
  613.6 35.4 %reduce-scatter.35.cloned.1.call-done = bf16[128,256]{1,0:T(8,128)(2,1)} async-done(((bf16[1024,256]{1,0:T(8,128)(2,1)}), bf16[128,256]{1,0:T(8,128)(2,1)}) %reduce-scatter.35.cloned.1.call-update) | async-done | bytes 65552
  650.7 44.2 %reduce-scatter.27.cloned.1.call-done = bf16[256,1024]{1,0:T(8,128)(2,1)} async-done(((bf16[1024,1024]{1,0:T(8,128)(2,1)}), bf16[256,1024]{1,0:T(8,128)(2,1)}) %reduce-scatter.27.cloned.1.call-update) | async-done | bytes 524304 | tf_op jit(solution)/shard_map/reduce_scatter | solution.py:208
  694.9 2.2 convert_add_fusion
  (168 shorter events, 35.3 us)
Async XLA Ops:
  8.0 51.1 %all-gather.7.cloned.1.call-start = ((), (), s32[]{:S(2)}) async-start(), calls=%async_computation.10 | async-start | bytes 2621440 | tf_op jit(solution)/shard_map/all_gather | solution.py:138
  8.8 117.2 %reduce-scatter.21.cloned.1.call-start = ((), (), s32[]{:S(2)}) async-start(), calls=%async_computation.11 | async-start | bytes 2621440 | tf_op jit(solution)/shard_map/reduce_scatter | solution.py:150
  21.7 39.7 %copy-start.11 = (bf16[1024,256]{1,0:T(8,128)(2,1)}, bf16[1024,256]{1,0:T(8,128)(2,1)S(1)}, u32[]{:S(2)}) copy-start(bf16[1024,256]{1,0:T(8,128)(2,1)S(1)} %all_gather.31) | copy-start | bytes 1572868
  31.2 31.2 %copy-start.13 = (bf16[1024,256]{1,0:T(8,128)(2,1)}, bf16[1024,256]{1,0:T(8,128)(2,1)S(1)}, u32[]{:S(2)}) copy-start(bf16[1024,256]{1,0:T(8,128)(2,1)S(1)} %all_gather.32) | copy-start | bytes 1572868
  40.4 24.4 %copy-start.9 = (bf16[1024,256]{1,0:T(8,128)(2,1)}, bf16[1024,256]{1,0:T(8,128)(2,1)S(1)}, u32[]{:S(2)}) copy-start(bf16[1024,256]{1,0:T(8,128)(2,1)S(1)} %all_gather.33) | copy-start | bytes 1572868
  68.0 13.1 %copy-start.18 = (bf16[256,1024]{1,0:T(8,128)(2,1)S(1)}, bf16[256,1024]{1,0:T(8,128)(2,1)}, u32[]{:S(2)}) copy-start(bf16[256,1024]{1,0:T(8,128)(2,1)} %all_gather.34) | copy-start | bytes 1572868
  80.4 3.4 copy-start.20
  80.4 3.4 copy-start.21
  80.4 3.4 copy-start.22
  80.4 45.5 %copy-start = (bf16[256,1024]{1,0:T(8,128)(2,1)S(1)}, bf16[256,1024]{1,0:T(8,128)(2,1)}, u32[]{:S(2)}) copy-start(bf16[256,1024]{1,0:T(8,128)(2,1)} %param.21) | copy-start | bytes 1572868
  81.1 49.7 %copy-start.19 = (bf16[32,8,2,512]{3,1,2,0:T(8,128)(2,1)}, bf16[32,8,2,512]{3,1,2,0:T(8,128)(2,1)S(1)}, u32[]{:S(2)}) copy-start(bf16[32,8,2,512]{3,1,2,0:T(8,128)(2,1)S(1)} %copy.74) | copy-start | bytes 1572868
  83.1 48.8 %copy-start.23 = (bf16[1024]{0:T(1024)(128)(2,1)S(1)}, bf16[1024]{0:T(1024)(128)(2,1)}, u32[]{:S(2)}) copy-start(bf16[1024]{0:T(1024)(128)(2,1)} %param.31) | copy-start | bytes 6148
  83.2 48.8 %all-gather.11.cloned.1.call-start = ((), (), s32[]{:S(2)}) async-start(), calls=%async_computation.13 | async-start | bytes 2359296 | tf_op jit(solution)/shard_map/all_gather | solution.py:134
  83.8 92.0 %all-gather.9.cloned.1.call-start = ((), (), s32[]{:S(2)}) async-start(), calls=%async_computation.12 | async-start | bytes 2621440 | tf_op jit(solution)/shard_map/all_gather | solution.py:160
  130.8 73.7 %all-gather.13.cloned.1.call-start = ((), (), s32[]{:S(2)}) async-start(), calls=%async_computation.14 | async-start | bytes 2359296 | tf_op jit(solution)/shard_map/all_gather | solution.py:135
  131.4 123.2 %reduce-scatter.23.cloned.1.call-start = ((), (), s32[]{:S(2)}) async-start(), calls=%async_computation.15 | async-start | bytes 2621440 | tf_op jit(solution)/shard_map/reduce_scatter | solution.py:164
  204.5 6.0 copy-start.24
  204.5 6.1 copy-start.25
  204.5 6.1 copy-start.26
  204.5 50.0 %copy-start.2 = (bf16[256,1024]{1,0:T(8,128)(2,1)S(1)}, bf16[256,1024]{1,0:T(8,128)(2,1)}, u32[]{:S(2)}) copy-start(bf16[256,1024]{1,0:T(8,128)(2,1)} %reduce-scatter.21.cloned.1.call-done) | copy-start | bytes 1572868
  210.5 45.9 %copy-start.17 = (bf16[256,1024]{1,0:T(8,128)(2,1)S(1)}, bf16[256,1024]{1,0:T(8,128)(2,1)}, u32[]{:S(2)}) copy-start(bf16[256,1024]{1,0:T(8,128)(2,1)} %param.37) | copy-start | bytes 1572868
  210.5 94.6 %all-gather.15.cloned.1.call-start = ((), (), s32[]{:S(2)}) async-start(), calls=%async_computation.16 | async-start | bytes 2621440 | tf_op jit(solution)/shard_map/all_gather | solution.py:173
  260.1 101.4 %reduce-scatter.25.cloned.1.call-start = ((), (), s32[]{:S(2)}) async-start(), calls=%async_computation.17 | async-start | bytes 2621440 | tf_op jit(solution)/shard_map/reduce_scatter | solution.py:180
  305.1 9.8 %copy-start.27 = (bf16[1024,1024]{1,0:T(8,128)(2,1)S(1)}, bf16[1024,1024]{1,0:T(8,128)(2,1)}, u32[]{:S(2)}) copy-start(bf16[1024,1024]{1,0:T(8,128)(2,1)} %all-gather.11.cloned.1.call-done) | copy-start | bytes 6291460
  313.6 1.4 copy-start.28
  318.7 93.2 %all-gather.17.cloned.1.call-start = ((), (), s32[]{:S(2)}) async-start(), calls=%async_computation.18 | async-start | bytes 2621440 | tf_op jit(solution)/shard_map/all_gather | solution.py:191
  365.0 1.0 copy-start.4
  366.9 100.9 %reduce-scatter.39.cloned.1.call-start = ((), (), s32[]{:S(2)}) async-start(), calls=%async_computation.25 | async-start | bytes 2359296
  374.2 125.6 %reduce-scatter.29.cloned.1.call-start = ((), (), s32[]{:S(2)}) async-start(), calls=%async_computation.20 | async-start | bytes 2359296 | tf_op jit(solution)/shard_map/reduce_scatter | solution.py:233
  380.3 164.2 %reduce-scatter.37.cloned.1.call-start = ((), (), s32[]{:S(2)}) async-start(), calls=%async_computation.24 | async-start | bytes 589824
  425.6 148.8 %reduce-scatter.31.cloned.1.call-start = ((), (), s32[]{:S(2)}) async-start(), calls=%async_computation.21 | async-start | bytes 589824
  426.4 1.3 copy-start.1
  432.9 1.8 copy-start.6
  436.1 1.0 copy-start.7
  437.1 1.3 copy-start.1
  443.6 1.8 copy-start.6
  446.8 1.0 copy-start.7
  449.5 3.6 copy-start.15
  453.0 158.9 %reduce-scatter.33.cloned.1.call-start = ((), (), s32[]{:S(2)}) async-start(), calls=%async_computation.22 | async-start | bytes 589824
  455.5 4.6 copy-start.14
  456.5 192.5 %reduce-scatter.35.cloned.1.call-start = ((), (), s32[]{:S(2)}) async-start(), calls=%async_computation.23 | async-start | bytes 589824
  459.0 4.1 copy-start.12
  459.1 4.1 copy-start.16
  460.1 3.8 copy-start.10
  462.8 232.1 %reduce-scatter.27.cloned.1.call-start = ((), (), s32[]{:S(2)}) async-start(), calls=%async_computation.19 | async-start | bytes 2621440 | tf_op jit(solution)/shard_map/reduce_scatter | solution.py:208
  463.2 2.4 copy-start.3
  467.6 33.9 %copy-start.8 = (bf16[2,512,4,64]{1,3,2,0:T(8,128)(2,1)S(1)}, bf16[2,512,4,64]{1,3,2,0:T(8,128)(2,1)}, u32[]{:S(2)}) copy-start(bf16[2,512,4,64]{1,3,2,0:T(8,128)(2,1)} %get-tuple-element.101) | copy-start | bytes 1572868
  467.6 227.3 %copy-start.5 = (f32[256,1024]{1,0:T(8,128)S(1)}, f32[256,1024]{1,0:T(8,128)}, u32[]{:S(2)}) copy-start(f32[256,1024]{1,0:T(8,128)} %copy-done.4) | copy-start | bytes 3145732
Sparse Core Ops, SparseCore 0:
  10.4 48.6 all-gather.6
  83.3 42.5 reduce-scatter.20
  210.6 43.8 reduce-scatter.22
  318.8 42.6 reduce-scatter.24
Sparse Core Ops, SparseCore 1:
  85.7 26.4 all-gather.10
  130.9 44.8 all-gather.8
  177.7 26.8 all-gather.12
  260.2 44.8 all-gather.14
  367.0 44.9 all-gather.16
  415.6 39.9 reduce-scatter.38
  458.7 41.1 reduce-scatter.28
  503.0 34.1 reduce-scatter.36
  540.1 34.1 reduce-scatter.30
  577.7 34.1 reduce-scatter.32
  614.9 34.1 reduce-scatter.34
  651.4 43.5 reduce-scatter.26
where the time goes:
time: 714 us; the launch traced here: 705 us
  waiting for transfers between devices  446 us (62%)
  matrix products  99.1 us (14%)
  blocking collectives  81.9 us (11%)
  local copies, waits for them, and re-layouts  30.4 us (4%)
  other arithmetic  29.1 us (4%)
  between operations  16.4 us (2%)
    unnamed x21, waiting for transfers between devices  101 us
    all_gather x1, waiting for transfers between devices, body(): lax.all_gather(summed_grad.astype(jnp.bfloat16), 'tensor', axis=0, tiled=...  44.8 us
    reduce_scatter x1, waiting for transfers between devices, body(): lax.psum_scatter((product_last(query_low, query_back) * scaling + product...  44.2 us
    reduce_scatter x1, waiting for transfers between devices, body(): lax.psum_scatter(product(hidden, shrink_full).astype(jnp.bfloat16), 'tens...  43.9 us
    all_gather x1, waiting for transfers between devices, body(): lax.all_gather(first_norm.astype(jnp.bfloat16), 'tensor', axis=0, tiled=T...  43.8 us
    reduce_scatter x1, waiting for transfers between devices, body(): lax.psum_scatter(product_last(expanded_low, expand_back).astype(jnp.bfloa...  42.8 us
    reduce_scatter x1, waiting for transfers between devices, body(): lax.psum_scatter(product(mixture, mixing_full).astype(jnp.bfloat16), 'ten...  42.1 us
    psum x1, blocking collectives, body(): lax.psum((gain_first, shift_first, gain_second, shift_second, mixing_sum,...  40.7 us
  transfers between devices with their start and end apart: 16, of which 13 were waited for; matrix products, arithmetic and copies ran while one was open for 14% of the time, Pallas kernels for 0%

commit v1 on v0

--- a/solution.py
+++ b/solution.py
@@ -7,6 +7,18 @@
 EPSILON = 1e-05
 CONTRACT_ROWS = (((0,), (0,)), ((), ()))
 CONTRACT_LAST = (((1,), (1,)), ((), ()))
+
+
+def doubled_up(x, axis, dim):
+    ways, here = (lax.axis_size(axis), lax.axis_index(axis))
+    grown, reach = (x, 1)
+    while reach < ways:
+        theirs = lax.ppermute(grown, axis, [(d, d ^ reach) for d in range(ways)])
+        mine_first = jnp.concatenate([grown, theirs], axis=dim)
+        theirs_first = jnp.concatenate([theirs, grown], axis=dim)
+        grown = jnp.where(here & reach == 0, mine_first, theirs_first)
+        reach = 2 * reach
+    return grown
 
 
 def layer_norm(inputs, gain, shift):
@@ -188,7 +200,7 @@
     shrink_sum = jnp.sum(summed_grad, axis=0)
     attended_grad, gain_first, shift_first = first_back(first_grad)
     mixing_sum = jnp.sum(attended_grad, axis=0)
-    attended_rows = lax.all_gather(attended_grad.astype(jnp.bfloat16), "tensor", axis=0, tiled=True)
+    attended_rows = doubled_up(attended_grad.astype(jnp.bfloat16), "tensor", 0)
     mixing_local = product_rows(mixture, attended_rows)
     mixture_low = product_last(attended_rows, mixing_back).astype(jnp.bfloat16)
     query_low, key_low, value_low = attend_backward(

time: 714 us -> 665 us (0.931)
  waiting for transfers between devices: 446 us -> 391 us
    ppermute x0 -> x2, waiting for transfers between devices: none -> 59 us  [doubled_up(): theirs = lax.ppermute(grown, axis, [(d, d ^ reach) for d in range(ways)])]
    unnamed x21 -> x20, waiting for transfers between devices: 101 us -> 64.3 us
    all_gather x1 -> x0, waiting for transfers between devices: 31.3 us -> none  [body(): lax.all_gather(attended_grad.astype(jnp.bfloat16), 'tensor', axis=0, tile...]
    reduce_scatter x1, waiting for transfers between devices: 29.9 us -> 0.01 us  [body(): lax.psum_scatter(expand_local.astype(jnp.bfloat16), 'dp', scatter_dimensi...]
    reduce_scatter x1, waiting for transfers between devices: 42.8 us -> 26.5 us  [body(): lax.psum_scatter(product_last(expanded_low, expand_back).astype(jnp.bfloa...]
    unnamed x71 -> x75, local copies, waits for them, and re-layouts: 21.5 us -> 22.7 us
  transfers between devices with their start and end apart: 16 -> 17, of which waited for: 13 -> 12; matrix products, arithmetic and copies ran while one was open for 14% -> 17% of each run, Pallas kernels for 0% -> 0%
where the time goes in v1:
time: 665 us; the launch traced here: 656 us
  waiting for transfers between devices  391 us (59%)
  matrix products  102 us (15%)
  blocking collectives  80.8 us (12%)
  local copies, waits for them, and re-layouts  31.6 us (5%)
  other arithmetic  30.3 us (5%)
  between operations  16.7 us (3%)
    unnamed x20, waiting for transfers between devices  64.3 us
    ppermute x2, waiting for transfers between devices, doubled_up(): theirs = lax.ppermute(grown, axis, [(d, d ^ reach) for d in range(ways)])  59 us
    all_gather x1, waiting for transfers between devices, body(): lax.all_gather(summed_grad.astype(jnp.bfloat16), 'tensor', axis=0, tiled=...  44.7 us
    reduce_scatter x1, waiting for transfers between devices, body(): lax.psum_scatter((product_last(query_low, query_back) * scaling + product...  44.6 us
    all_gather x1, waiting for transfers between devices, body(): lax.all_gather(first_norm.astype(jnp.bfloat16), 'tensor', axis=0, tiled=T...  44.1 us
    reduce_scatter x1, waiting for transfers between devices, body(): lax.psum_scatter(product(hidden, shrink_full).astype(jnp.bfloat16), 'tens...  43.9 us
    reduce_scatter x1, waiting for transfers between devices, body(): lax.psum_scatter(product(mixture, mixing_full).astype(jnp.bfloat16), 'ten...  42.1 us
    psum x1, blocking collectives, body(): lax.psum((gain_first, shift_first, gain_second, shift_second, mixing_sum,...  39.6 us
  transfers between devices with their start and end apart: 17, of which 12 were waited for; matrix products, arithmetic and copies ran while one was open for 17% of the time, Pallas kernels for 0%

profile of v1, /device:TPU:0, one launch (start us, length us, event | category | flops | bytes accessed | tf_op | source)
XLA Modules:
  0.0 656.2 jit_solution(8691400540521905568)
XLA Ops:
  10.1 11.6 %all_gather.28 = bf16[1024,256]{1,0:T(8,128)(2,1)S(1)} all-gather(bf16[128,256]{1,0:T(8,128)(2,1)} %param.22), channel_id=1, replica_groups=mesh['dp'=8,'tensor'=4] {'dp'}, dimensions={0}, use_global_device_ids=true | all-gather | bytes 589824 | tf_op jit(solution)/shard_map/all_gather | solution.py:142
  21.7 9.5 %all_gather.29 = bf16[1024,256]{1,0:T(8,128)(2,1)S(1)} all-gather(bf16[128,256]{1,0:T(8,128)(2,1)} %param.23), channel_id=1, replica_groups=mesh['dp'=8,'tensor'=4] {'dp'}, dimensions={0}, use_global_device_ids=true | all-gather | bytes 589824 | tf_op jit(solution)/shard_map/all_gather | solution.py:143
  31.3 9.2 %all_gather.30 = bf16[1024,256]{1,0:T(8,128)(2,1)S(1)} all-gather(bf16[128,256]{1,0:T(8,128)(2,1)} %param.24), channel_id=1, replica_groups=mesh['dp'=8,'tensor'=4] {'dp'}, dimensions={0}, use_global_device_ids=true | all-gather | bytes 589824 | tf_op jit(solution)/shard_map/all_gather | solution.py:144
  40.4 10.9 %all_gather.31 = bf16[256,1024]{1,0:T(8,128)(2,1)} all-gather(bf16[256,128]{1,0:T(8,128)(2,1)} %param.25), channel_id=1, replica_groups=mesh['dp'=8,'tensor'=4] {'dp'}, dimensions={1}, use_global_device_ids=true | all-gather | bytes 589824 | tf_op jit(solution)/shard_map/all_gather | solution.py:145
  51.3 7.7 %all-gather.6.cloned.1.call-done = bf16[1024,1024]{1,0:T(8,128)(2,1)} async-done(((bf16[256,1024]{1,0:T(8,128)(2,1)}), bf16[1024,1024]{1,0:T(8,128)(2,1)}) %all-gather.6.cloned.1.call-update) | async-done | bytes 2097168 | tf_op jit(solution)/shard_map/all_gather | solution.py:150
  59.1 2.3 fusion.43
  62.5 2.3 convolution_convert_fusion.10
  64.8 3.1 fusion.44
  68.0 12.4 %while.27 = (s32[]{:T(128)}, bf16[2,512,4,64]{1,3,2,0:T(8,128)(2,1)S(1)}, f32[2,4,512]{2,1,0:T(4,128)S(1)}, bf16[2,512,4,64]{1,3,2,0:T(8,128)(2,1)S(1)}, bf16[10...) while((s32[]{:T(128)}, bf16[2,512,4,64]{1,3,2,0:T(8,128)(2,1)S(1)}, ...), condition=%wide.region_3.4_spmd, body=%wide.region_0.3_spmd.sunk | while | flops 549582848 | bytes 26804320 | solution.py:62
  68.1 1.4 fusion.129
  69.4 1.7 fusion.130
  71.2 3.0 fusion.131
  75.6 1.7 fusion.130
  77.4 3.0 fusion.131
  81.1 2.1 convolution_convert_fusion.5
  83.9 42.1 %reduce-scatter.21.cloned.1.call-done = bf16[256,1024]{1,0:T(8,128)(2,1)} async-done(((bf16[1024,1024]{1,0:T(8,128)(2,1)}), bf16[256,1024]{1,0:T(8,128)(2,1)}) %reduce-scatter.21.cloned.1.call-update) | async-done | bytes 524304 | tf_op jit(solution)/shard_map/reduce_scatter | solution.py:162
  128.6 2.2 fusion.55
  131.7 44.1 %all-gather.8.cloned.1.call-done = bf16[1024,1024]{1,0:T(8,128)(2,1)} async-done(((bf16[256,1024]{1,0:T(8,128)(2,1)}), bf16[1024,1024]{1,0:T(8,128)(2,1)}) %all-gather.8.cloned.1.call-update) | async-done | bytes 2097168 | tf_op jit(solution)/shard_map/all_gather | solution.py:172
  175.8 14.9 %multiply_convert_fusion.1 = (bf16[1024,1024]{1,0:T(8,128)(2,1)}, f32[1024,1024]{1,0:T(8,128)}, f32[1024,1024]{1,0:T(8,128)}) fusion(f32[1024]{0:T(1024)S(1)} %convert_element_type.190, bf16[1024,1024]{1,0:T(8,128)(2,1)} %all-gather.8.cloned.1.call-done, bf16[1024,1024]{1,0:T(8,128)(2,1)} %all-gather.10.cloned.1.call-done), kind=kOutput, calls=%fused_computation.45 | convolution fusion | flops 2216689664 | bytes 14684160 | tf_op jit(solution)/shard_map/dot_general | solution.py:31
  190.7 13.8 %all-gather.12.cloned.1.call-done = bf16[1024,1024]{1,0:T(8,128)(2,1)} async-done(((bf16[1024,128]{1,0:T(8,128)(2,1)}), bf16[1024,1024]{1,0:T(8,128)(2,1)}) %all-gather.12.cloned.1.call-update) | async-done | bytes 2097168 | tf_op jit(solution)/shard_map/all_gather | solution.py:147
  204.5 5.9 convolution_convert_fusion.4
  210.6 43.9 %reduce-scatter.23.cloned.1.call-done = bf16[256,1024]{1,0:T(8,128)(2,1)} async-done(((bf16[1024,1024]{1,0:T(8,128)(2,1)}), bf16[256,1024]{1,0:T(8,128)(2,1)}) %reduce-scatter.23.cloned.1.call-update) | async-done | bytes 524304 | tf_op jit(solution)/shard_map/reduce_scatter | solution.py:176
  254.5 1.6 fusion.63
  257.4 2.3 fusion.62
  260.9 44.7 %all-gather.14.cloned.1.call-done = bf16[1024,1024]{1,0:T(8,128)(2,1)} async-done(((bf16[256,1024]{1,0:T(8,128)(2,1)}), bf16[1024,1024]{1,0:T(8,128)(2,1)}) %all-gather.14.cloned.1.call-update) | async-done | bytes 2097168 | tf_op jit(solution)/shard_map/all_gather | solution.py:185
  305.7 8.5 %convert_reduce_fusion = (f32[1024]{0:T(1024)S(1)}, bf16[1024,1024]{1,0:T(8,128)(2,1)S(1)}) fusion(f32[1024,1024]{1,0:T(8,128)} %get-tuple-element.287, f32[1024,1024]{1,0:T(8,128)} %get-tuple-element.297, f32[1024]{0:T(1024)S(1)} %convert_element_type.190, bf16[1024,1024]{1,0:T(8,128)(2,1)} %all-gather.14.cloned.1.call-done, ...), kind=kOutput, calls=%fused_computation.42 | convolution fusion | flops 2165308416 | bytes 14688256 | tf_op jit(solution)/shard_map/dot_general | solution.py:39
  315.5 3.7 convolution_convert_fusion.3
  319.3 5.9 convolution_convert_fusion.1
  325.2 3.9 copy.70
  329.2 6.0 convolution_convert_fusion.2
  335.5 26.5 %reduce-scatter.25.cloned.1.call-done = bf16[256,1024]{1,0:T(8,128)(2,1)} async-done(((bf16[1024,1024]{1,0:T(8,128)(2,1)}), bf16[256,1024]{1,0:T(8,128)(2,1)}) %reduce-scatter.25.cloned.1.call-update) | async-done | bytes 524304 | tf_op jit(solution)/shard_map/reduce_scatter | solution.py:192
  362.1 1.7 multiply_reduce_fusion.1
  363.8 1.7 fusion.61
  366.7 13.5 %collective-permute-done = bf16[256,1024]{1,0:T(8,128)(2,1)S(1)} collective-permute-done((bf16[256,1024]{1,0:T(8,128)(2,1)S(1)}, bf16[256,1024]{1,0:T(8,128)(2,1)S(1)}, u32[]{:S(2)}, u32[]{:S(2)}) %collective-permute-start) | collective-permute-done | bytes 524320 | tf_op jit(solution)/shard_map/ppermute | solution.py:16
  380.2 1.5 maximum_select_fusion.1
  381.7 2.0 collective-permute-start.1
  383.6 45.5 %collective-permute-done.1 = bf16[512,1024]{1,0:T(8,128)(2,1)} collective-permute-done((bf16[512,1024]{1,0:T(8,128)(2,1)}, bf16[512,1024]{1,0:T(8,128)(2,1)}, u32[]{:S(2)}, u32[]{:S(2)}) %collective-permute-start.1) | collective-permute-done | bytes 1048608 | tf_op jit(solution)/shard_map/ppermute | solution.py:16
  429.2 4.2 convolution_convert_fusion.6
  433.4 2.0 copy.68
  435.4 4.0 convolution_convert_fusion.9
  439.5 2.8 reshape.191
  442.2 2.3 copy.55
  445.4 21.4 %while.28 = (s32[]{:T(128)}, f32[1024,4,64]{0,2,1:T(8,128)S(1)}, f32[1024,4,64]{0,2,1:T(8,128)S(1)}, bf16[2,512,4,64]{1,3,2,0:T(8,128)(2,1)}, bf16[2,512,4,64]{1...) while((s32[]{:T(128)}, f32[1024,4,64]{0,2,1:T(8,128)S(1)}, ...), condition=%wide.region_17.18_spmd.clone, body=%wide.region_15.17_spmd.clone.sunk | while | flops 1362229248 | bytes 76341480 | solution.py:98
  446.7 1.8 fusion.143
  448.5 3.3 multiply_reduce_fusion.6
  451.9 1.8 multiply_convert_fusion.3
  453.6 1.4 fusion.144
  457.4 1.8 fusion.143
  459.2 3.3 multiply_reduce_fusion.6
  462.6 1.8 multiply_convert_fusion.3
  464.3 1.4 fusion.144
  466.8 1.6 copy.56
  468.4 2.5 fusion.48
  472.4 2.3 fusion.49
  476.0 2.3 fusion.50
  479.4 2.7 fusion.67
  483.0 1.4 copy-done.3
  484.4 2.1 add_convert_fusion
  488.7 1.8 convert_element_type.221
  490.9 39.6 %all-reduce = (f32[1024]{0:T(1024)S(1)}, f32[1024]{0:T(1024)S(1)}, f32[1024]{0:T(1024)}, f32[4096]{0:T(1024)S(1)}, f32[1024]{0:T(1024)}, /*index=5*/f32[1024]{0:...) all-reduce(f32[1024]{0:T(1024)S(1)} %bitcast.173, ...), channel_id=1, replica_groups=mesh['dp'=8,'tensor'=4] {'dp','tensor'}, use_global_device_ids=true, to_apply=%region_26.27 | all-reduce | flops 12288 | bytes 98304 | tf_op jit(solution)/shard_map/psum | solution.py:258
  535.7 27.1 %reduce-scatter.33.cloned.1.call-done = bf16[128,256]{1,0:T(8,128)(2,1)} async-done(((bf16[1024,256]{1,0:T(8,128)(2,1)}), bf16[128,256]{1,0:T(8,128)(2,1)}) %reduce-scatter.33.cloned.1.call-update) | async-done | bytes 65552
  564.5 35.3 %reduce-scatter.35.cloned.1.call-done = bf16[128,256]{1,0:T(8,128)(2,1)} async-done(((bf16[1024,256]{1,0:T(8,128)(2,1)}), bf16[128,256]{1,0:T(8,128)(2,1)}) %reduce-scatter.35.cloned.1.call-update) | async-done | bytes 65552
  601.6 44.6 %reduce-scatter.27.cloned.1.call-done = bf16[256,1024]{1,0:T(8,128)(2,1)} async-done(((bf16[1024,1024]{1,0:T(8,128)(2,1)}), bf16[256,1024]{1,0:T(8,128)(2,1)}) %reduce-scatter.27.cloned.1.call-update) | async-done | bytes 524304 | tf_op jit(solution)/shard_map/reduce_scatter | solution.py:220
  646.1 2.2 convert_add_fusion
  (174 shorter events, 36.3 us)
Async XLA Ops:
  8.0 51.1 %all-gather.6.cloned.1.call-start = ((), (), s32[]{:S(2)}) async-start(), calls=%async_computation.10 | async-start | bytes 2621440 | tf_op jit(solution)/shard_map/all_gather | solution.py:150
  8.8 117.2 %reduce-scatter.21.cloned.1.call-start = ((), (), s32[]{:S(2)}) async-start(), calls=%async_computation.11 | async-start | bytes 2621440 | tf_op jit(solution)/shard_map/reduce_scatter | solution.py:162
  21.7 39.7 %copy-start.11 = (bf16[1024,256]{1,0:T(8,128)(2,1)}, bf16[1024,256]{1,0:T(8,128)(2,1)S(1)}, u32[]{:S(2)}) copy-start(bf16[1024,256]{1,0:T(8,128)(2,1)S(1)} %all_gather.28) | copy-start | bytes 1572868
  31.2 31.2 %copy-start.13 = (bf16[1024,256]{1,0:T(8,128)(2,1)}, bf16[1024,256]{1,0:T(8,128)(2,1)S(1)}, u32[]{:S(2)}) copy-start(bf16[1024,256]{1,0:T(8,128)(2,1)S(1)} %all_gather.29) | copy-start | bytes 1572868
  40.4 24.4 %copy-start.9 = (bf16[1024,256]{1,0:T(8,128)(2,1)}, bf16[1024,256]{1,0:T(8,128)(2,1)S(1)}, u32[]{:S(2)}) copy-start(bf16[1024,256]{1,0:T(8,128)(2,1)S(1)} %all_gather.30) | copy-start | bytes 1572868
  68.0 13.1 %copy-start.18 = (bf16[256,1024]{1,0:T(8,128)(2,1)S(1)}, bf16[256,1024]{1,0:T(8,128)(2,1)}, u32[]{:S(2)}) copy-start(bf16[256,1024]{1,0:T(8,128)(2,1)} %all_gather.31) | copy-start | bytes 1572868
  80.4 3.4 copy-start.22
  80.4 3.4 copy-start.23
  80.4 3.4 copy-start.24
  80.4 45.5 %copy-start = (bf16[256,1024]{1,0:T(8,128)(2,1)S(1)}, bf16[256,1024]{1,0:T(8,128)(2,1)}, u32[]{:S(2)}) copy-start(bf16[256,1024]{1,0:T(8,128)(2,1)} %param.21) | copy-start | bytes 1572868
  81.1 49.7 %copy-start.19 = (bf16[32,8,2,512]{3,1,2,0:T(8,128)(2,1)}, bf16[32,8,2,512]{3,1,2,0:T(8,128)(2,1)S(1)}, u32[]{:S(2)}) copy-start(bf16[32,8,2,512]{3,1,2,0:T(8,128)(2,1)S(1)} %copy.74) | copy-start | bytes 1572868
  83.2 48.4 %copy-start.25 = (bf16[1024]{0:T(1024)(128)(2,1)S(1)}, bf16[1024]{0:T(1024)(128)(2,1)}, u32[]{:S(2)}) copy-start(bf16[1024]{0:T(1024)(128)(2,1)} %param.31) | copy-start | bytes 6148
  83.2 48.5 %all-gather.10.cloned.1.call-start = ((), (), s32[]{:S(2)}) async-start(), calls=%async_computation.13 | async-start | bytes 2359296 | tf_op jit(solution)/shard_map/all_gather | solution.py:146
  83.8 92.0 %all-gather.8.cloned.1.call-start = ((), (), s32[]{:S(2)}) async-start(), calls=%async_computation.12 | async-start | bytes 2621440 | tf_op jit(solution)/shard_map/all_gather | solution.py:172
  130.8 73.7 %all-gather.12.cloned.1.call-start = ((), (), s32[]{:S(2)}) async-start(), calls=%async_computation.14 | async-start | bytes 2359296 | tf_op jit(solution)/shard_map/all_gather | solution.py:147
  131.4 123.1 %reduce-scatter.23.cloned.1.call-start = ((), (), s32[]{:S(2)}) async-start(), calls=%async_computation.15 | async-start | bytes 2621440 | tf_op jit(solution)/shard_map/reduce_scatter | solution.py:176
  204.5 6.0 copy-start.26
  204.5 6.0 copy-start.27
  204.5 6.0 copy-start.28
  204.5 50.0 %copy-start.2 = (bf16[256,1024]{1,0:T(8,128)(2,1)S(1)}, bf16[256,1024]{1,0:T(8,128)(2,1)}, u32[]{:S(2)}) copy-start(bf16[256,1024]{1,0:T(8,128)(2,1)} %reduce-scatter.21.cloned.1.call-done) | copy-start | bytes 1572868
  210.5 45.9 %copy-start.17 = (bf16[256,1024]{1,0:T(8,128)(2,1)S(1)}, bf16[256,1024]{1,0:T(8,128)(2,1)}, u32[]{:S(2)}) copy-start(bf16[256,1024]{1,0:T(8,128)(2,1)} %param.37) | copy-start | bytes 1572868
  210.5 95.2 %all-gather.14.cloned.1.call-start = ((), (), s32[]{:S(2)}) async-start(), calls=%async_computation.16 | async-start | bytes 2621440 | tf_op jit(solution)/shard_map/all_gather | solution.py:185
  260.7 101.4 %reduce-scatter.25.cloned.1.call-start = ((), (), s32[]{:S(2)}) async-start(), calls=%async_computation.17 | async-start | bytes 2621440 | tf_op jit(solution)/shard_map/reduce_scatter | solution.py:192
  305.7 9.8 %copy-start.29 = (bf16[1024,1024]{1,0:T(8,128)(2,1)S(1)}, bf16[1024,1024]{1,0:T(8,128)(2,1)}, u32[]{:S(2)}) copy-start(bf16[1024,1024]{1,0:T(8,128)(2,1)} %all-gather.10.cloned.1.call-done) | copy-start | bytes 6291460
  314.1 1.3 copy-start.30
  319.2 167.4 %reduce-scatter.39.cloned.1.call-start = ((), (), s32[]{:S(2)}) async-start(), calls=%async_computation.24 | async-start | bytes 2359296
  329.2 159.5 %reduce-scatter.29.cloned.1.call-start = ((), (), s32[]{:S(2)}) async-start(), calls=%async_computation.19 | async-start | bytes 2359296 | tf_op jit(solution)/shard_map/reduce_scatter | solution.py:245
  335.2 197.1 %reduce-scatter.37.cloned.1.call-start = ((), (), s32[]{:S(2)}) async-start(), calls=%async_computation.23 | async-start | bytes 589824
  365.5 1.0 copy-start.4
  366.7 13.5 %collective-permute-start = (bf16[256,1024]{1,0:T(8,128)(2,1)S(1)}, bf16[256,1024]{1,0:T(8,128)(2,1)S(1)}, u32[]{:S(2)}, u32[]{:S(2)}) collective-permute-start(bf16[256,1024]{1,0:T(8,128)(2,1)S(1)} %get-tuple-element.294), channel_id=1, source_target_pairs={{0,1},{1,0},{2,3},{3,2},{4,5},{5,4},{6,7},{7,6},{8,9},{9,8},{10,11... | collective-permute-start | bytes 1572872 | tf_op jit(solution)/shard_map/ppermute | solution.py:16
  381.7 47.5 %collective-permute-start.1 = (bf16[512,1024]{1,0:T(8,128)(2,1)}, bf16[512,1024]{1,0:T(8,128)(2,1)}, u32[]{:S(2)}, u32[]{:S(2)}) collective-permute-start(bf16[512,1024]{1,0:T(8,128)(2,1)} %maximum_select_fusion.1), channel_id=1, source_target_pairs={{0,2},{1,3},{2,0},{3,1},{4,6},{5,7},{6,4},{7,5},{8,10},{9,11},{10,... | collective-permute-start | bytes 3145736 | tf_op jit(solution)/shard_map/ppermute | solution.py:16
  444.5 89.5 %reduce-scatter.31.cloned.1.call-start = ((), (), s32[]{:S(2)}) async-start(), calls=%async_computation.20 | async-start | bytes 589824
  445.4 1.3 copy-start.1
  451.8 1.8 copy-start.6
  455.0 1.0 copy-start.7
  456.1 1.3 copy-start.1
  462.5 1.8 copy-start.6
  465.7 1.0 copy-start.7
  468.4 3.9 copy-start.15
  472.0 90.8 %reduce-scatter.33.cloned.1.call-start = ((), (), s32[]{:S(2)}) async-start(), calls=%async_computation.21 | async-start | bytes 589824
  474.7 4.6 copy-start.14
  475.8 124.0 %reduce-scatter.35.cloned.1.call-start = ((), (), s32[]{:S(2)}) async-start(), calls=%async_computation.22 | async-start | bytes 589824
  478.3 3.9 copy-start.12
  478.3 3.9 copy-start.16
  479.4 3.6 copy-start.10
  482.1 164.0 %reduce-scatter.27.cloned.1.call-start = ((), (), s32[]{:S(2)}) async-start(), calls=%async_computation.18 | async-start | bytes 2621440 | tf_op jit(solution)/shard_map/reduce_scatter | solution.py:220
  482.2 2.2 copy-start.3
  486.5 4.0 copy-start.8
  486.5 4.4 copy-start.20
  486.5 4.4 copy-start.21
  486.5 159.6 %copy-start.5 = (f32[256,1024]{1,0:T(8,128)S(1)}, f32[256,1024]{1,0:T(8,128)}, u32[]{:S(2)}) copy-start(f32[256,1024]{1,0:T(8,128)} %copy-done.4) | copy-start | bytes 3145732
Sparse Core Ops, SparseCore 0:
  10.4 48.6 all-gather.5
  83.3 42.5 reduce-scatter.20
  210.6 43.8 reduce-scatter.22
  319.4 42.6 reduce-scatter.24
  365.6 40.5 reduce-scatter.38
  409.3 41.2 reduce-scatter.28
  453.9 34.1 reduce-scatter.36
  491.1 34.1 reduce-scatter.30
  528.7 34.0 reduce-scatter.32
  565.7 34.0 reduce-scatter.34
  602.2 43.8 reduce-scatter.26
Sparse Core Ops, SparseCore 1:
  85.7 26.4 all-gather.9
  130.9 44.8 all-gather.7
  177.7 26.8 all-gather.11
  260.7 44.8 all-gather.13
